TPU v7x, 128 devices: a whole 4x4x4 slice. The times are simulated.
128 devices in a mesh: dp: 16 (over z, y), tensor: 8 (over x, core).
Axes of the slice: x: 4, y: 4, z: 4, core: 2. Of those that a mesh axis runs over, the one named last changes fastest.
Arguments:
- acts: bfloat16 [24576, 6144], P('dp', 'tensor'), may hold values from -600 to 600, as said below
- grads_out: bfloat16 [24576, 24576], P('dp', 'tensor'), may hold values from -600 to 600, as said below
- sketch_in: bfloat16 [6144, 256], P('tensor'), may hold values from -0.078125 to 0.078125
- sketch_out: bfloat16 [24576, 256], P('tensor'), may hold values from -0.0390625 to 0.0390625
- weight_grad: float32 [6144, 24576], P('dp', 'tensor'), may hold values from -6 to 6
Outputs:
- precond: float32 [6144, 24576], P('dp', 'tensor')
Inputs may be any that keep to these rules, and one draw needn't show every extreme that they name: acts: rows and columns of varying scale. grads_out: rows and columns of varying scale.
All inputs are finite; a program needn't handle non-finite values.
Results may differ from a plain program's by a relative error of at most 0.0015.
Values sent between devices are 32-bit elements; how exact they have to be, the bound alone decides.
No kernel may reach another device: no remote copies, remote signals or barrier semaphores. Data moves between devices by JAX's collectives and lax.ppermute only.
A program may use at most 128 MiB of HBM per device.

v0:
```python
import jax
import jax.numpy as jnp
from jax import lax
from jax.sharding import PartitionSpec as P

D = 6144
FF = 24576


DAMPING = 0.1


def transpose_dot(left, right):
    return lax.dot_general(
        left, right, (((0,), (0,)), ((), ())), preferred_element_type=jnp.float32
    )


def precise_dot(left, right):
    return jnp.dot(left, right, precision=lax.Precision.HIGHEST)


def body(acts, grads_out, sketch_in, sketch_out, weight_grad):
    tokens_all = acts.shape[0] * lax.axis_size("dp")
    square_act = jnp.sum(jnp.square(acts.astype(jnp.float32)))
    square_grad = jnp.sum(jnp.square(grads_out.astype(jnp.float32)))
    part_act = jnp.dot(acts, sketch_in, preferred_element_type=jnp.float32)
    part_grad = jnp.dot(grads_out, sketch_out, preferred_element_type=jnp.float32)
    full_act, full_grad = lax.psum((part_act, part_grad), "tensor")
    core_act = precise_dot(full_act.T, full_act) / tokens_all
    core_grad = precise_dot(full_grad.T, full_grad) / tokens_all
    sketch_act = full_act.astype(jnp.bfloat16)
    sketch_grad = full_grad.astype(jnp.bfloat16)
    range_act = transpose_dot(acts, sketch_act) / tokens_all
    range_grad = transpose_dot(grads_out, sketch_grad) / tokens_all
    range_act, range_grad, core_act, core_grad, trace_act, trace_grad = lax.psum(
        (range_act, range_grad, core_act, core_grad, square_act, square_grad), "dp"
    )
    gram_grad = precise_dot(range_grad.T, range_grad)
    right_part = precise_dot(weight_grad, range_grad)
    right_sums, gram_grad, trace_act, trace_grad = lax.psum(
        (right_part, gram_grad, trace_act, trace_grad), "tensor"
    )
    damp_act = DAMPING * trace_act / (tokens_all * D)
    damp_grad = DAMPING * trace_grad / (tokens_all * FF)
    inner_grad = damp_grad * core_grad + gram_grad
    solved_grad = jax.scipy.linalg.cho_solve((jnp.linalg.cholesky(inner_grad), True), right_sums.T)
    halfway = (weight_grad - precise_dot(solved_grad.T, range_grad.T)) / damp_grad
    whole_act = lax.all_gather(range_act, "tensor", axis=0, tiled=True)
    gram_act = precise_dot(whole_act.T, whole_act)
    row_count = weight_grad.shape[0]
    rows_act = lax.dynamic_slice_in_dim(whole_act, lax.axis_index("dp") * row_count, row_count, 0)
    left_sums = lax.psum(precise_dot(rows_act.T, halfway), "dp")
    inner_act = damp_act * core_act + gram_act
    solved_act = jax.scipy.linalg.cho_solve((jnp.linalg.cholesky(inner_act), True), left_sums)
    return (halfway - precise_dot(rows_act, solved_act)) / damp_act


def solution(mesh):
    return jax.shard_map(
        body,
        mesh=mesh,
        in_specs=(
            P("dp", "tensor"),
            P("dp", "tensor"),
            P("tensor", None),
            P("tensor", None),
            P("dp", "tensor"),
        ),
        out_specs=P("dp", "tensor"),
        check_vma=False,
    )
```

profile of v0, /device:TPU:1, one launch (start us, length us, event | category | flops | bytes accessed | tf_op | source)
XLA Modules:
  0.0 565.3 jit_solution(11986781711932216307)
XLA Ops:
  6.5 1.4 copy-done
  7.9 7.6 %fusion.41 = f32[1536,256]{1,0:T(8,128)} fusion(bf16[1536,3072]{1,0:T(8,128)(2,1)} %param.7, bf16[3072,256]{1,0:T(8,128)(2,1)S(1)} %copy-done), kind=kOutput, calls=%fused_computation.87 | convolution fusion | flops 2415919104 | bytes 12582912 | tf_op jit(solution)/shard_map/dot_general | solution.py:28
  15.5 1.9 fusion.44
  17.5 0.0 all-reduce.14.cloned.1.call-start
  17.6 70.6 %all-reduce.18.cloned.1.call-done = (f32[1536,256]{1,0:T(8,128)}, f32[1536,256]{1,0:T(8,128)}) async-done(((f32[1536,256]{1,0:T(8,128)}, f32[1536,256]{1,0:T(8,128)}), (f32[1536,256]{1,0:T(8,128)}, f32[1536,256]{1,0:T(8,128)})) %all-reduce.18.cloned.1.call-update) | async-done | bytes 3145744 | tf_op jit(solution)/shard_map/psum | solution.py:29
  88.2 8.7 %fusion = f32[3072,256]{0,1:T(8,128)} fusion(bf16[1536,3072]{1,0:T(8,128)(2,1)} %param.7, f32[1536,256]{1,0:T(8,128)} %get-tuple-element.49), kind=kOutput, calls=%fused_computation.9 | convolution fusion | flops 2417098752 | bytes 14155776 | tf_op jit(solution)/shard_map/dot_general | solution.py:14
  96.9 3.3 convolution_multiply_fusion.3
  100.2 1.7 fusion.6
  102.0 0.2 all-reduce.16.cloned.1.call-start
  102.2 105.4 %all-reduce.14.cloned.1.call-done = (f32[3072,256]{0,1:T(8,128)}, f32[256,256]{0,1:T(8,128)}, f32[768,256]{0,1:T(8,128)}) async-done(((f32[3072,256]{0,1:T(8,128)}, f32[256,256]{0,1:T(8,128)}, f32[768,256]{0,1:T(8,128)}), (f32[3072,256]{0,1:T(8,128)}, f32[256,256]{0,1:T(8,128)}, f32[768,256]{0,1:T(8,128)})) %all-reduce.14.cloned.1.call-update) | async-done | bytes 4194320 | tf_op jit(solution)/shard_map/psum | solution.py:36
  207.7 6.4 %fusion.42 = f32[256,256]{0,1:T(8,128)} fusion(f32[3072,256]{0,1:T(8,128)} %get-tuple-element.42), kind=kOutput, calls=%fused_computation.88 | convolution fusion | flops 2415919104 | bytes 3407872 | tf_op jit(solution)/shard_map/dot_general | solution.py:20
  214.0 7.9 %fusion.43 = f32[256,384]{1,0:T(8,128)} fusion(f32[3072,256]{0,1:T(8,128)S(1)} %copy-done.5, f32[384,3072]{1,0:T(8,128)} %param.10), kind=kOutput, calls=%fused_computation.89 | convolution fusion | flops 3623878656 | bytes 8257536 | tf_op jit(solution)/shard_map/dot_general | solution.py:20
  222.0 0.5 all-gather.2.cloned.1.call-update
  222.6 9.3 %multiply_reduce_fusion = f32[]{:T(128)} fusion(bf16[1536,3072]{1,0:T(8,128)(2,1)} %param.7), kind=kLoop, calls=%fused_computation.4 | loop fusion | flops 14155775 | bytes 9437188 | tf_op jit(solution)/shard_map/reduce_sum | solution.py:26
  231.9 1.8 multiply_reduce_fusion.1
  233.7 32.0 %all-reduce.1 = (f32[]{:T(128)}, f32[]{:T(128)}) all-reduce(f32[]{:T(128)} %multiply_reduce_fusion, f32[]{:T(128)} %multiply_reduce_fusion.1), channel_id=1, replica_groups=mesh['dp'=16,'tensor'=8] {'dp'}, use_global_device_ids=true, to_apply=%region_1.0 | all-reduce | flops 2 | bytes 16 | tf_op jit(solution)/shard_map/psum | solution.py:36
  265.7 20.4 %all-reduce.4 = (f32[]{:T(128)}, f32[]{:T(128)}) all-reduce(f32[]{:T(128)} %get-tuple-element.38, f32[]{:T(128)} %get-tuple-element.39), channel_id=1, replica_groups=mesh['dp'=16,'tensor'=8] {'tensor'}, use_global_device_ids=true, to_apply=%region_2.0 | all-reduce | flops 2 | bytes 16 | tf_op jit(solution)/shard_map/psum | solution.py:41
  286.7 3.3 convolution_multiply_fusion.2
  290.0 1.0 multiply_add_fusion
  291.1 0.1 copy.8
  291.2 11.7 %cholesky.130 = f32[128,128]{1,0:T(8,128)S(1)} custom-call(f32[128,128]{1,0:T(8,128)S(1)} %cholesky.194), custom_call_target="Cholesky" | custom-call | tf_op jit(solution)/shard_map/jit(cholesky)/cholesky | solution.py:47
  303.0 9.8 %custom-call.25 = f32[1,128,128]{1,2,0:T(8,128)S(1)} custom-call(f32[1,128,128]{2,1,0:T(8,128)S(1)} %get-tuple-element.62), custom_call_target="InvertDiagBlocksLowerTriangular" | custom-call | tf_op jit(solution)/shard_map/jit(cholesky)/cholesky | solution.py:47
  312.8 0.2 constant_dynamic-update-slice_fusion.3
  313.1 0.3 convolution_subtract_fusion.5
  313.3 12.2 %cholesky.147 = f32[128,128]{1,0:T(8,128)S(1)} custom-call(f32[128,128]{1,0:T(8,128)S(1)} %convolution_subtract_fusion.5), custom_call_target="Cholesky" | custom-call | tf_op jit(solution)/shard_map/jit(cholesky)/cholesky | solution.py:47
  325.5 0.6 compare_reduce_fusion.2
  327.4 0.1 triangular_solve.114
  327.5 3.9 while.2
  327.6 0.6 fusion.79
  328.1 1.3 bitcast_dynamic-update-slice_fusion.4
  329.5 0.6 fusion.79
  330.1 1.3 bitcast_dynamic-update-slice_fusion.4
  331.4 19.7 %custom-call.22 = f32[2,128,128]{1,2,0:T(8,128)S(1)} custom-call(f32[2,128,128]{2,1,0:T(8,128)S(1)} %get-tuple-element.13), custom_call_target="InvertDiagBlocksLowerTriangular" | custom-call | tf_op jit(solution)/shard_map/jit(_cho_solve)/triangular_solve | solution.py:47
  351.1 0.4 fusion.17
  351.5 0.3 convolution_subtract_fusion.3
  351.8 0.4 fusion.27
  352.2 0.3 fusion.26
  352.5 0.4 convolution_subtract_fusion.2
  352.9 0.3 fusion.25
  353.2 9.2 %subtract_divide_fusion.1 = f32[384,3072]{1,0:T(8,128)} fusion(f32[384,3072]{1,0:T(8,128)} %param.10, f32[3072,256]{0,1:T(8,128)} %get-tuple-element.42, f32[]{:T(128)S(6)} %div.46, f32[128,384]{1,0:T(8,128)S(1)} %fusion.26, f32[128,384]{1,0:T(8,128)S(1)} %fusion.25), kind=kOutput, calls=%fused_computation.7 | convolution fusion | flops 3626336256 | bytes 12976132 | tf_op jit(solution)/shard_map/dot_general | solution.py:20
  362.4 8.3 %fusion.13 = f32[256,3072]{1,0:T(8,128)} fusion(f32[384,3072]{1,0:T(8,128)} %subtract_divide_fusion.1, f32[6144,256]{0,1:T(8,128)} %all-gather.2.cloned.1.call-done, s32[]{:T(128)S(6)} %select_n.6), kind=kOutput, calls=%fused_computation.32 | convolution fusion | flops 3623878656 | bytes 8257540 | tf_op jit(solution)/shard_map/dot_general | solution.py:20
  371.3 90.6 %all-reduce.12.cloned.1.call-done = (f32[256,3072]{1,0:T(8,128)}, f32[256,256]{0,1:T(8,128)}) async-done(((f32[256,3072]{1,0:T(8,128)}, f32[256,256]{0,1:T(8,128)}), (f32[256,3072]{1,0:T(8,128)}, f32[256,256]{0,1:T(8,128)})) %all-reduce.12.cloned.1.call-update) | async-done | bytes 3407888 | tf_op jit(solution)/shard_map/psum | solution.py:53
  461.9 17.4 %convolution_add_fusion = f32[256,256]{0,1:T(8,128)S(1)} fusion(f32[6144,256]{0,1:T(8,128)} %all-gather.2.cloned.1.call-done, f32[256,256]{0,1:T(8,128)} %get-tuple-element.41, f32[]{:T(128)S(6)} %div.56), kind=kOutput, calls=%fused_computation.21 | convolution fusion | flops 4831969280 | bytes 6815748 | tf_op jit(solution)/shard_map/dot_general | solution.py:20
  479.3 0.1 copy.11
  479.5 11.7 %cholesky.164 = f32[128,128]{1,0:T(8,128)S(1)} custom-call(f32[128,128]{1,0:T(8,128)S(1)} %cholesky.197), custom_call_target="Cholesky" | custom-call | tf_op jit(solution)/shard_map/jit(cholesky)/cholesky | solution.py:55
  491.3 9.8 %custom-call.26 = f32[1,128,128]{1,2,0:T(8,128)S(1)} custom-call(f32[1,128,128]{2,1,0:T(8,128)S(1)} %get-tuple-element.58), custom_call_target="InvertDiagBlocksLowerTriangular" | custom-call | tf_op jit(solution)/shard_map/jit(cholesky)/cholesky | solution.py:55
  501.1 0.2 constant_dynamic-update-slice_fusion.1
  501.3 0.3 convolution_subtract_fusion.4
  501.6 11.7 %cholesky.181 = f32[128,128]{1,0:T(8,128)S(1)} custom-call(f32[128,128]{1,0:T(8,128)S(1)} %convolution_subtract_fusion.4), custom_call_target="Cholesky" | custom-call | tf_op jit(solution)/shard_map/jit(cholesky)/cholesky | solution.py:55
  513.3 0.7 compare_reduce_fusion
  514.0 0.7 compare_reduce_fusion.1
  515.9 4.0 while.3
  516.0 0.6 fusion.80
  516.6 1.3 bitcast_dynamic-update-slice_fusion.5
  518.0 0.6 fusion.80
  518.6 1.3 bitcast_dynamic-update-slice_fusion.5
  520.0 19.9 %custom-call.23 = f32[2,128,128]{1,2,0:T(8,128)S(1)} custom-call(f32[2,128,128]{2,1,0:T(8,128)S(1)} %get-tuple-element.21), custom_call_target="InvertDiagBlocksLowerTriangular" | custom-call | tf_op jit(solution)/shard_map/jit(_cho_solve)/triangular_solve | solution.py:55
  539.9 2.9 fusion.4
  542.7 2.9 convolution_subtract_fusion.1
  545.6 1.5 fusion.30
  547.1 1.5 fusion.29
  548.6 1.5 convolution_subtract_fusion
  550.1 1.5 fusion.28
  551.6 6.9 %subtract_divide_fusion = f32[384,3072]{1,0:T(8,128)} fusion(f32[384,3072]{1,0:T(8,128)S(1)} %bitcast.95, f32[128,3072]{1,0:T(8,128)S(1)} %fusion.29, f32[128,3072]{1,0:T(8,128)S(1)} %fusion.28, f32[]{:T(128)S(6)} %div.56, f32[6144,256]{0,1:T(8,128)} %all-gather.2.cloned.1.call-done, s32[]{:T(128)S(6)} %select_n.6), kind=kOutput, calls=%fused_computation.5 | convolution fusion | flops 3627024384 | bytes 12976136 | tf_op jit(solution)/shard_map/dot_general | solution.py:20
  (54 shorter events, 0.6 us)
Async XLA Ops:
  6.5 1.4 copy-start
  6.5 9.0 %copy-start.9 = (bf16[768,256]{1,0:T(8,128)(2,1)S(1)}, bf16[768,256]{1,0:T(8,128)(2,1)}, u32[]{:S(2)}) copy-start(bf16[768,256]{1,0:T(8,128)(2,1)} %param.8) | copy-start | bytes 1179652
  6.5 81.7 %all-reduce.18.cloned.1.call-start = ((), (), s32[]{:S(2)}) async-start(), calls=%async_computation.4 | async-start | bytes 6291456 | tf_op jit(solution)/shard_map/psum | solution.py:29
  7.9 7.6 %copy-start.2 = (bf16[1536,768]{1,0:T(8,128)(2,1)S(1)}, bf16[1536,768]{1,0:T(8,128)(2,1)}, u32[]{:S(2)}) copy-start(bf16[1536,768]{1,0:T(8,128)(2,1)} %param.6) | copy-start | bytes 7077892
  17.5 190.1 %all-reduce.14.cloned.1.call-start = ((), (), s32[]{:S(2)}) async-start(), calls=%async_computation.2 | async-start | bytes 8388608 | tf_op jit(solution)/shard_map/psum | solution.py:36
  88.2 8.7 %copy-start.6 = (f32[1536,256]{1,0:T(8,128)S(1)}, f32[1536,256]{1,0:T(8,128)}, u32[]{:S(2)}) copy-start(f32[1536,256]{1,0:T(8,128)} %get-tuple-element.49) | copy-start | bytes 4718596
  88.2 12.0 %copy-start.7 = (f32[1536,256]{1,0:T(8,128)S(1)}, f32[1536,256]{1,0:T(8,128)}, u32[]{:S(2)}) copy-start(f32[1536,256]{1,0:T(8,128)} %get-tuple-element.50) | copy-start | bytes 4718596
  96.9 3.3 copy-start.3
  102.0 188.0 %all-reduce.16.cloned.1.call-start = ((), (), s32[]{:S(2)}) async-start(), calls=%async_computation.3 | async-start | bytes 1310720 | tf_op jit(solution)/shard_map/psum | solution.py:41
  207.7 6.4 %copy-start.5 = (f32[3072,256]{0,1:T(8,128)S(1)}, f32[3072,256]{0,1:T(8,128)}, u32[]{:S(2)}) copy-start(f32[3072,256]{0,1:T(8,128)} %get-tuple-element.42) | copy-start | bytes 9437188
  221.9 140.4 %all-gather.2.cloned.1.call-start = ((), (), s32[]{:S(2)}) async-start(), calls=%async_computation | async-start | bytes 7077888 | tf_op jit(solution)/shard_map/all_gather | solution.py:49
  222.5 239.4 %all-reduce.12.cloned.1.call-start = ((), (), s32[]{:S(2)}) async-start(), calls=%async_computation.1 | async-start | bytes 6815744 | tf_op jit(solution)/shard_map/psum | solution.py:53
  222.6 9.3 %copy-start.4 = (bf16[1536,768]{1,0:T(8,128)(2,1)S(1)}, bf16[1536,768]{1,0:T(8,128)(2,1)}, u32[]{:S(2)}) copy-start(bf16[1536,768]{1,0:T(8,128)(2,1)} %param.6) | copy-start | bytes 7077892
  231.9 58.1 %copy-start.10 = (f32[256,256]{0,1:T(8,128)S(1)}, f32[256,256]{0,1:T(8,128)}, u32[]{:S(2)}) copy-start(f32[256,256]{0,1:T(8,128)} %get-tuple-element.43) | copy-start | bytes 786436
  290.0 61.1 %copy-start.8 = (f32[256,384]{1,0:T(8,128)S(1)}, f32[256,384]{1,0:T(8,128)}, u32[]{:S(2)}) copy-start(f32[256,384]{1,0:T(8,128)} %get-tuple-element.47) | copy-start | bytes 1179652
  547.1 4.5 slice-start
  548.6 3.0 slice-start.1
  551.6 6.9 %copy-start.1 = (bf16[3072,256]{1,0:T(8,128)(2,1)S(1)}, bf16[3072,256]{1,0:T(8,128)(2,1)}, u32[]{:S(2)}) copy-start(bf16[3072,256]{1,0:T(8,128)(2,1)} %param.9) | copy-start | bytes 4718596
Sparse Core Ops, SparseCore 0:
  17.6 70.5 all-reduce.17
  102.1 105.5 all-reduce.13
  222.1 59.0 all-reduce.15
  282.7 42.7 all-gather.1
  370.8 91.0 all-reduce.11
where the time goes:
time: 572 us; the launch traced here: 565 us
  waiting for transfers between devices  267 us (47%)
  other arithmetic  121 us (21%)
  matrix products  97.2 us (17%)
  blocking collectives  52.4 us (9%)
  between operations  17.4 us (3%)
  local copies, waits for them, and re-layouts  9.62 us (2%)
    psum x1, waiting for transfers between devices, body(): lax.psum((range_act, range_grad, core_act, core_grad, square_act, square_...  105 us
    psum x1, waiting for transfers between devices, body(): left_sums = lax.psum(precise_dot(rows_act.T, halfway), 'dp')  90.6 us
    psum x1, waiting for transfers between devices, body(): full_act, full_grad = lax.psum((part_act, part_grad), 'tensor')  70.6 us
    dot_general x8, matrix products, precise_dot(): return jnp.dot(left, right, precision=lax.Precision.HIGHEST)  62.6 us
    another operation x7, other arithmetic, body(): jnp.linalg.cholesky(inner_act)  34.6 us
    another operation x6, other arithmetic, body(): jnp.linalg.cholesky(inner_grad)  34.4 us
    psum x1, blocking collectives, body(): lax.psum((range_act, range_grad, core_act, core_grad, square_act, square_...  32 us
    psum x1, blocking collectives, body(): lax.psum((right_part, gram_grad, trace_act, trace_grad), 'tensor')  20.4 us
  transfers between devices with their start and end apart: 5, of which 3 were waited for; matrix products, arithmetic and copies ran while one was open for 15% of the time, Pallas kernels for 0%

commit v1 on v0

v1 whole, which is shorter than its diff:
```python
import jax
import jax.numpy as jnp
from jax import lax
from jax.sharding import PartitionSpec as P

D = 6144
FF = 24576
R = 256

DAMPING = 0.1


def ring(kind, step):
    if kind == "y":
        return [(i, i // 4 * 4 + (i % 4 + step) % 4) for i in range(16)]
    if kind == "z":
        return [(i, (i // 4 + step) % 4 * 4 + i % 4) for i in range(16)]
    return [(i, (i // 2 + step) % 4 * 2 + i % 2) for i in range(8)]


def send(value, kind, step):
    return lax.ppermute(value, "tensor" if kind == "x" else "dp", ring(kind, step))


def swap_cores(value):
    return lax.ppermute(value, "tensor", [(i, i ^ 1) for i in range(8)])


def place(kind):
    if kind == "y":
        return lax.axis_index("dp") % 4
    if kind == "z":
        return lax.axis_index("dp") // 4
    return lax.axis_index("tensor") // 2


def rows(value, index, count):
    return lax.dynamic_slice_in_dim(value, index * count, count, 0)


def scatter_four(value, kind):
    here, count = place(kind), value.shape[0] // 4
    two, one, three = (
        send(rows(value, (here + step) % 4, count), kind, step) for step in (2, 1, 3)
    )
    return (rows(value, here, count) + two) + (one + three)


def gather_four(value, kind):
    here, count = place(kind), value.shape[0]
    parts = {step: send(value, kind, step) for step in (2, 1, 3)}
    whole = jnp.zeros((4 * count,) + value.shape[1:], value.dtype)
    whole = lax.dynamic_update_slice_in_dim(whole, value, here * count, 0)
    for step in (1, 3, 2):
        whole = lax.dynamic_update_slice_in_dim(
            whole, parts[step], (here - step) % 4 * count, 0
        )
    return whole


def sum_four(value, kind):
    two, one, three = (send(value, kind, step) for step in (2, 1, 3))
    return (value + two) + (one + three)


def scatter_dp(first, second):
    first, second = scatter_four(first, "y"), scatter_four(second, "z")
    return scatter_four(first, "z"), scatter_four(second, "y")


def gather_dp(first, second):
    first, second = gather_four(first, "z"), gather_four(second, "y")
    return gather_four(first, "y"), gather_four(second, "z")


def sum_dp(value):
    return sum_four(sum_four(value, "y"), "z")


def tensor_chunk():
    index = lax.axis_index("tensor")
    return index % 2 * 4 + index // 2


def scatter_tensor(value):
    core, half = lax.axis_index("tensor") % 2, value.shape[0] // 2
    other = swap_cores(rows(value, 1 - core, half))
    return scatter_four(rows(value, core, half) + other, "x")


def gather_tensor(value):
    core = lax.axis_index("tensor") % 2
    value = gather_four(value, "x")
    other = swap_cores(value)
    low = jnp.where(core == 0, value, other)
    high = jnp.where(core == 0, other, value)
    return jnp.concatenate([low, high])


def contract(left, right, dims, precision=lax.Precision.HIGH):
    return lax.dot_general(
        left, right, (dims, ((), ())), precision=precision, preferred_element_type=jnp.float32
    )


def inverse_factor(inner):
    factor = jnp.linalg.cholesky(inner)
    return lax.linalg.triangular_solve(
        factor, jnp.eye(R, dtype=jnp.float32), left_side=True, lower=True
    )


def body(acts, grads_out, sketch_in, sketch_out, weight_grad):
    tokens_all = acts.shape[0] * lax.axis_size("dp")
    chunk = tensor_chunk()
    width = R // 8

    full_grad = gather_tensor(
        scatter_tensor(jnp.dot(grads_out, sketch_out, preferred_element_type=jnp.float32))
    )
    full_act = gather_tensor(
        scatter_tensor(jnp.dot(acts, sketch_in, preferred_element_type=jnp.float32))
    )
    square_grad = jnp.sum(jnp.square(grads_out.astype(jnp.float32)))
    square_act = jnp.sum(jnp.square(acts.astype(jnp.float32)))
    core_grad = contract(full_grad, full_grad, ((0,), (0,))) / tokens_all
    core_act = contract(full_act, full_act, ((0,), (0,))) / tokens_all

    part = contract(full_grad.astype(jnp.bfloat16), grads_out, ((0,), (0,)), None) / tokens_all
    extra = jnp.concatenate(
        [
            rows(core_grad, chunk, width).T,
            jnp.full((R, 1), square_grad),
            jnp.zeros((R, 128 - width - 1), jnp.float32),
        ],
        axis=1,
    )
    part = jnp.concatenate([part, extra], axis=1)
    range_grad = jnp.concatenate(gather_dp(*scatter_dp(part[: R // 2], part[R // 2 :])))
    extra = range_grad[:, 3072:]
    range_grad = range_grad[:, :3072]

    part = contract(acts, full_act.astype(jnp.bfloat16), ((0,), (0,)), None) / tokens_all
    part = part.reshape(4, 4, 2, 24, R)
    first, second = scatter_dp(
        part[:, :, 0].transpose(1, 0, 2, 3).reshape(384, R), part[:, :, 1].reshape(384, R)
    )
    piece = jnp.concatenate([first, second])
    moves = []
    for d in range(16):
        for t in range(8):
            k = d % 8
            moves.append((d * 8 + t, (2 * t + d // 8) * 8 + 2 * (k % 4) + k // 4))
    piece = lax.ppermute(piece, ("dp", "tensor"), moves)
    rows_act = gather_tensor(piece)

    part = contract(rows_act, weight_grad, ((0,), (0,)))
    left_sums = jnp.concatenate(gather_dp(*scatter_dp(part[: R // 2], part[R // 2 :])))

    gram = contract(rows_act, rows_act, ((0,), (0,)))
    small = jnp.concatenate(
        [
            rows(gram, chunk, width),
            rows(core_act, chunk, width),
            jnp.full((8, R), square_act),
        ]
    )
    small = gather_tensor(sum_dp(small)).reshape(8, 72, R)
    gram_act = small[:, :32].reshape(R, R)
    core_act = small[:, 32:64].reshape(R, R)
    damp_act = DAMPING * jnp.sum(small[:, 64, 0]) / (tokens_all * D)
    inverse_act = inverse_factor(damp_act * core_act + gram_act)

    right = contract(weight_grad, range_grad, ((1,), (1,)))
    gram = contract(range_grad, range_grad, ((1,), (1,)))
    part = jnp.concatenate([right.reshape(8, 48, R), gram.reshape(8, 32, R)], axis=1)
    part = scatter_tensor(part.reshape(640, R))
    part = jnp.concatenate(
        [part, extra[:, :width].T, jnp.full((8, R), extra[0, width])]
    )
    part = gather_tensor(part).reshape(8, 120, R)
    right_sums = part[:, :48].reshape(384, R)
    gram_grad = part[:, 48:80].reshape(R, R)
    core_grad = part[:, 80:112].reshape(R, R)
    damp_grad = DAMPING * jnp.sum(part[:, 112, 0]) / (tokens_all * FF)
    inverse_grad = inverse_factor(damp_grad * core_grad + gram_grad)

    both = contract(rows_act, right_sums, ((0,), (0,)))
    both = gather_tensor(sum_dp(rows(both, chunk, width)))

    solved_act = contract(
        contract(rows_act, inverse_act, ((1,), (1,))), inverse_act, ((1,), (0,))
    )
    right_sums = right_sums - contract(solved_act, both, ((1,), (0,)))
    solved_grad = contract(
        contract(right_sums, inverse_grad, ((1,), (1,))), inverse_grad, ((1,), (0,))
    )
    out = weight_grad - contract(solved_grad, range_grad, ((1,), (0,)))
    out = out - contract(solved_act, left_sums, ((1,), (0,)))
    return out / (damp_act * damp_grad)


def solution(mesh):
    return jax.shard_map(
        body,
        mesh=mesh,
        in_specs=(
            P("dp", "tensor"),
            P("dp", "tensor"),
            P("tensor", None),
            P("tensor", None),
            P("dp", "tensor"),
        ),
        out_specs=P("dp", "tensor"),
        check_vma=False,
    )
```

time: 572 us -> 740 us (1.29)
  local copies, waits for them, and re-layouts: 9.62 us -> 289 us
  waiting for transfers between devices: 267 us -> 69.1 us
  starting transfers between devices: 0.34 us -> 182 us
  blocking collectives: 52.4 us -> 0 us
  matrix products: 97.2 us -> 45.5 us
  other arithmetic: 121 us -> 134 us
  between operations: 17.4 us -> 7.13 us
    psum x4 -> x0, waiting for transfers between devices: 267 us -> none  [the longest x1 105 us: body(): lax.psum((range_act, range_grad, core_act, core_grad, square_act, square_...]
    dynamic_update_slice x0 -> x52, local copies, waits for them, and re-layouts: none -> 211 us  [the longest x44 165 us: gather_four(): lax.dynamic_update_slice_in_dim(whole, parts[step], (here - step) % 4 * c...]
    ppermute x0 -> x109, starting transfers between devices: none -> 182 us  [the longest x99 136 us: send(): lax.ppermute(value, 'tensor' if kind == 'x' else 'dp', ring(kind, step))]
    ppermute x0 -> x109, waiting for transfers between devices: none -> 69.1 us  [the longest x99 66.8 us: send(): lax.ppermute(value, 'tensor' if kind == 'x' else 'dp', ring(kind, step))]
    psum x2 -> x0, blocking collectives: 52.4 us -> none  [the longest x1 32 us: body(): lax.psum((range_act, range_grad, core_act, core_grad, square_act, square_...]
    dot_general x11 -> x17, matrix products: 75 us -> 37.5 us  [the longest x16 36.7 us: contract(): lax.dot_general(left, right, (dims, ((), ())), precision=precision, prefe...]
    ppermute x0 -> x15, local copies, waits for them, and re-layouts: none -> 34.7 us  [send(): lax.ppermute(value, 'tensor' if kind == 'x' else 'dp', ring(kind, step))]
    another operation x16 -> x10, matrix products: 14.7 us -> 2.7 us  [the longest x6 1.75 us: inverse_factor(): lax.linalg.triangular_solve(factor, jnp.eye(R, dtype=jnp.float32), left_s...]
  transfers between devices with their start and end apart: 5 -> 109, of which waited for: 3 -> 30; matrix products, arithmetic and copies ran while one was open for 15% -> 60% of each run, Pallas kernels for 0% -> 0%
where the time goes in v1:
time: 740 us; the launch traced here: 727 us
  local copies, waits for them, and re-layouts  289 us (39%)
  starting transfers between devices  182 us (25%)
  other arithmetic  134 us (18%)
  waiting for transfers between devices  69.1 us (9%)
  matrix products  45.5 us (6%)
    dynamic_update_slice x44, local copies, waits for them, and re-layouts, gather_four(): lax.dynamic_update_slice_in_dim(whole, parts[step], (here - step) % 4 * c...  165 us
    ppermute x99, starting transfers between devices, send(): lax.ppermute(value, 'tensor' if kind == 'x' else 'dp', ring(kind, step))  136 us
    another operation x14, other arithmetic, inverse_factor(): factor = jnp.linalg.cholesky(inner)  69.2 us
    ppermute x99, waiting for transfers between devices, send(): lax.ppermute(value, 'tensor' if kind == 'x' else 'dp', ring(kind, step))  66.8 us
    dynamic_update_slice x8, local copies, waits for them, and re-layouts, gather_four(): whole = lax.dynamic_update_slice_in_dim(whole, value, here * count, 0)  46.5 us
    another operation x5, other arithmetic, inverse_factor(): lax.linalg.triangular_solve(factor, jnp.eye(R, dtype=jnp.float32), left_s...  39.4 us
    ppermute x9, starting transfers between devices, swap_cores(): return lax.ppermute(value, 'tensor', [(i, i ^ 1) for i in range(8)])  37.9 us
    dot_general x16, matrix products, contract(): lax.dot_general(left, right, (dims, ((), ())), precision=precision, prefe...  36.7 us
  transfers between devices with their start and end apart: 109, of which 30 were waited for; matrix products, arithmetic and copies ran while one was open for 60% of the time, Pallas kernels for 0%

profile of v1, /device:TPU:1, one launch (start us, length us, event | category | flops | bytes accessed | tf_op | source)
XLA Modules:
  0.0 726.6 jit_solution(5835618910101668843)
XLA Ops:
  1.4 5.3 fusion.66
  15.3 2.9 collective-permute-start.41
  20.9 9.1 %multiply_reduce_fusion = f32[]{:T(128)} fusion(bf16[1536,3072]{1,0:T(8,128)(2,1)} %param.9), kind=kLoop, calls=%fused_computation.4 | loop fusion | flops 14155775 | bytes 9437188 | tf_op jit(solution)/shard_map/reduce_sum | solution.py:124
  37.2 5.1 collective-permute-done.2
  43.1 4.5 collective-permute-done.44
  49.6 3.9 collective-permute-start.47
  58.5 5.0 collective-permute-done.5
  72.9 4.4 convolution_multiply_fusion
  77.8 3.0 collective-permute-start.48
  83.5 3.7 collective-permute-start.54
  88.6 4.3 concatenate.43
  109.7 6.8 collective-permute-start.9
  117.1 8.3 %collective-permute-start.60 = (f32[48,256]{1,0:T(8,128)S(1)}, f32[48,256]{1,0:T(8,128)S(1)}, u32[]{:S(2)}, u32[]{:S(2)}) collective-permute-start(f32[48,256]{1,0:T(8,128)S(1)} %pad_maximum_fusion.18), channel_id=1, source_target_pairs={{0,0},{1,16},{2,32},{3,48},{4,64},{5,80},{6,96},{7,112},{8,2},{9,1... | collective-permute-start | bytes 147464 | tf_op jit(solution)/shard_map/ppermute | solution.py:154
  127.1 5.7 collective-permute-done.61
  137.3 3.0 collective-permute-done.63
  140.2 5.9 collective-permute-start.22
  146.2 5.3 collective-permute-start.64
  157.8 3.1 fusion.21
  186.6 12.7 %dynamic_update_slice.172 = f32[32,3200]{0,1:T(8,128)S(1)} dynamic-update-slice(f32[32,3200]{0,1:T(8,128)S(1)} %broadcast.121.clone.1, f32[8,3200]{0,1:T(8,128)} %copy.33, s32[]{:T(128)S(6)} %select_n.662, s32[]{:T(128)} %copy.143) | dynamic-update-slice | bytes 204804 | tf_op jit(solution)/shard_map/dynamic_update_slice | solution.py:53
  200.5 8.9 %dynamic_update_slice.180 = f32[32,3200]{0,1:T(8,128)} dynamic-update-slice(f32[32,3200]{0,1:T(8,128)} %broadcast.121.clone, f32[8,3200]{0,1:T(8,128)} %copy.43, s32[]{:T(128)S(6)} %select_n.685, s32[]{:T(128)} %copy.143) | dynamic-update-slice | bytes 204804 | tf_op jit(solution)/shard_map/dynamic_update_slice | solution.py:53
  210.2 3.8 collective-permute-start.85
  225.5 14.2 %dynamic_update_slice.173 = f32[32,3200]{0,1:T(8,128)S(1)} dynamic-update-slice(f32[32,3200]{0,1:T(8,128)S(1)} %dynamic_update_slice.172, f32[8,3200]{0,1:T(8,128)} %copy.34, s32[]{:T(128)S(6)} %select_n.670, s32[]{:T(128)} %copy.143) | dynamic-update-slice | bytes 204804 | tf_op jit(solution)/shard_map/dynamic_update_slice | solution.py:55
  242.2 14.2 %dynamic_update_slice.174 = f32[32,3200]{0,1:T(8,128)S(1)} dynamic-update-slice(f32[32,3200]{0,1:T(8,128)S(1)} %dynamic_update_slice.173, f32[8,3200]{0,1:T(8,128)} %copy.35, s32[]{:T(128)S(6)} %select_n.672, s32[]{:T(128)} %copy.143) | dynamic-update-slice | bytes 204804 | tf_op jit(solution)/shard_map/dynamic_update_slice | solution.py:55
  259.0 14.2 %dynamic_update_slice.175 = f32[32,3200]{0,1:T(8,128)S(1)} dynamic-update-slice(f32[32,3200]{0,1:T(8,128)S(1)} %dynamic_update_slice.174, f32[8,3200]{0,1:T(8,128)} %copy.36, s32[]{:T(128)S(6)} %select_n.674, s32[]{:T(128)} %copy.143) | dynamic-update-slice | bytes 204804 | tf_op jit(solution)/shard_map/dynamic_update_slice | solution.py:55
  275.8 12.7 %dynamic_update_slice.176 = f32[128,3200]{0,1:T(8,128)S(1)} dynamic-update-slice(f32[128,3200]{0,1:T(8,128)S(1)} %broadcast.120.clone.1, f32[32,3200]{0,1:T(8,128)} %copy-done.8, s32[]{:T(128)S(6)} %select_n.654, s32[]{:T(128)} %copy.143) | dynamic-update-slice | bytes 819204 | tf_op jit(solution)/shard_map/dynamic_update_slice | solution.py:53
  291.0 10.3 %dynamic_update_slice.181 = f32[32,3200]{0,1:T(8,128)} dynamic-update-slice(f32[32,3200]{0,1:T(8,128)} %dynamic_update_slice.180, f32[8,3200]{0,1:T(8,128)} %copy.44, s32[]{:T(128)S(6)} %select_n.689, s32[]{:T(128)} %copy.143) | dynamic-update-slice | bytes 204804 | tf_op jit(solution)/shard_map/dynamic_update_slice | solution.py:55
  303.9 10.3 %dynamic_update_slice.182 = f32[32,3200]{0,1:T(8,128)} dynamic-update-slice(f32[32,3200]{0,1:T(8,128)} %dynamic_update_slice.181, f32[8,3200]{0,1:T(8,128)} %copy.45, s32[]{:T(128)S(6)} %select_n.690, s32[]{:T(128)} %copy.143) | dynamic-update-slice | bytes 204804 | tf_op jit(solution)/shard_map/dynamic_update_slice | solution.py:55
  316.7 10.3 %dynamic_update_slice.183 = f32[32,3200]{0,1:T(8,128)} dynamic-update-slice(f32[32,3200]{0,1:T(8,128)} %dynamic_update_slice.182, f32[8,3200]{0,1:T(8,128)} %copy.46, s32[]{:T(128)S(6)} %select_n.691, s32[]{:T(128)} %copy.143) | dynamic-update-slice | bytes 204804 | tf_op jit(solution)/shard_map/dynamic_update_slice | solution.py:55
  331.0 8.9 %dynamic_update_slice.184 = f32[128,3200]{0,1:T(8,128)} dynamic-update-slice(f32[128,3200]{0,1:T(8,128)} %broadcast.120.clone, f32[32,3200]{0,1:T(8,128)} %dynamic_update_slice.183, s32[]{:T(128)S(6)} %select_n.681, s32[]{:T(128)} %copy.143) | dynamic-update-slice | bytes 819204 | tf_op jit(solution)/shard_map/dynamic_update_slice | solution.py:53
  341.5 4.3 collective-permute-start.97
  352.1 3.1 collective-permute-start.99
  360.1 5.4 collective-permute-done.99
  365.5 3.0 collective-permute-start.90
  377.1 10.6 %collective-permute-start.74 = (f32[288,256]{1,0:T(8,128)}, f32[288,256]{1,0:T(8,128)S(1)}, u32[]{:S(2)}, u32[]{:S(2)}) collective-permute-start(f32[288,256]{1,0:T(8,128)} %constant_dynamic-update-slice_fusion.22), channel_id=1, source_target_pairs={{0,1},{1,0},{2,3},{3,2},{4,5},{5,4},{6,7},{7,6},{8,9},{9,8},{10,11... | collective-permute-start | bytes 884744 | tf_op jit(solution)/shard_map/ppermute | solution.py:26
  392.1 11.7 %cholesky.130 = f32[128,128]{1,0:T(8,128)S(1)} custom-call(f32[128,128]{1,0:T(8,128)S(1)} %cholesky.194), custom_call_target="Cholesky" | custom-call | tf_op jit(solution)/shard_map/jit(cholesky)/cholesky | solution.py:107
  403.9 9.8 %custom-call.13 = f32[1,128,128]{1,2,0:T(8,128)S(1)} custom-call(f32[1,128,128]{2,1,0:T(8,128)S(1)} %get-tuple-element.125), custom_call_target="InvertDiagBlocksLowerTriangular" | custom-call | tf_op jit(solution)/shard_map/jit(cholesky)/cholesky | solution.py:107
  414.2 11.7 %cholesky.147 = f32[128,128]{1,0:T(8,128)S(1)} custom-call(f32[128,128]{1,0:T(8,128)S(1)} %convolution_subtract_fusion.4), custom_call_target="Cholesky" | custom-call | tf_op jit(solution)/shard_map/jit(cholesky)/cholesky | solution.py:107
  428.5 4.0 while.4
  432.4 19.7 %custom-call.14 = f32[2,128,128]{1,2,0:T(8,128)S(1)} custom-call(f32[2,128,128]{2,1,0:T(8,128)S(1)} %get-tuple-element.21), custom_call_target="InvertDiagBlocksLowerTriangular" | custom-call | tf_op jit(solution)/shard_map/triangular_solve/custom-call.0 | solution.py:108
  454.5 3.0 collective-permute-start.92
  459.7 3.0 collective-permute-start.93
  465.2 4.4 collective-permute-done.103
  475.0 3.1 collective-permute-done.105
  478.0 3.3 collective-permute-start.30
  486.8 14.2 %dynamic_update_slice.177 = f32[128,3200]{0,1:T(8,128)S(1)} dynamic-update-slice(f32[128,3200]{0,1:T(8,128)S(1)} %dynamic_update_slice.176, f32[32,3200]{0,1:T(8,128)} %copy.38, s32[]{:T(128)S(6)} %select_n.676, s32[]{:T(128)} %copy.143) | dynamic-update-slice | bytes 819204 | tf_op jit(solution)/shard_map/dynamic_update_slice | solution.py:55
  503.8 14.2 %dynamic_update_slice.178 = f32[128,3200]{0,1:T(8,128)S(1)} dynamic-update-slice(f32[128,3200]{0,1:T(8,128)S(1)} %dynamic_update_slice.177, f32[32,3200]{0,1:T(8,128)} %copy.40, s32[]{:T(128)S(6)} %select_n.678, s32[]{:T(128)} %copy.143) | dynamic-update-slice | bytes 819204 | tf_op jit(solution)/shard_map/dynamic_update_slice | solution.py:55
  521.8 14.2 %dynamic_update_slice.179 = f32[128,3200]{0,1:T(8,128)S(1)} dynamic-update-slice(f32[128,3200]{0,1:T(8,128)S(1)} %dynamic_update_slice.178, f32[32,3200]{0,1:T(8,128)} %copy.42, s32[]{:T(128)S(6)} %select_n.680, s32[]{:T(128)} %copy.143) | dynamic-update-slice | bytes 819204 | tf_op jit(solution)/shard_map/dynamic_update_slice | solution.py:55
  539.7 10.3 %dynamic_update_slice.185 = f32[128,3200]{0,1:T(8,128)} dynamic-update-slice(f32[128,3200]{0,1:T(8,128)} %dynamic_update_slice.184, f32[32,3200]{0,1:T(8,128)} %copy.48, s32[]{:T(128)S(6)} %select_n.692, s32[]{:T(128)} %copy.143) | dynamic-update-slice | bytes 819204 | tf_op jit(solution)/shard_map/dynamic_update_slice | solution.py:55
  552.7 10.7 %dynamic_update_slice.186 = f32[128,3200]{0,1:T(8,128)} dynamic-update-slice(f32[128,3200]{0,1:T(8,128)} %dynamic_update_slice.185, f32[32,3200]{0,1:T(8,128)} %copy.50, s32[]{:T(128)S(6)} %select_n.693, s32[]{:T(128)} %copy.143) | dynamic-update-slice | bytes 819204 | tf_op jit(solution)/shard_map/dynamic_update_slice | solution.py:55
  565.1 10.3 %dynamic_update_slice.187 = f32[128,3200]{0,1:T(8,128)} dynamic-update-slice(f32[128,3200]{0,1:T(8,128)} %dynamic_update_slice.186, f32[32,3200]{0,1:T(8,128)} %copy.52, s32[]{:T(128)S(6)} %select_n.694, s32[]{:T(128)} %copy.143) | dynamic-update-slice | bytes 819204 | tf_op jit(solution)/shard_map/dynamic_update_slice | solution.py:55
  575.4 8.0 %convolution_bitcast_fusion = f32[384,256]{0,1:T(8,128)S(1)} fusion(f32[384,3072]{1,0:T(8,128)} %param.12, f32[128,3200]{0,1:T(8,128)S(1)} %dynamic_update_slice.179, f32[128,3200]{0,1:T(8,128)} %dynamic_update_slice.187), kind=kOutput, calls=%fused_computation.22 | convolution fusion | flops 1812725760 | bytes 8388608 | tf_op jit(solution)/shard_map/dot_general | solution.py:101
  588.0 7.3 %collective-permute-start.32 = (f32[320,256]{1,0:T(8,128)S(1)}, f32[320,256]{1,0:T(8,128)S(1)}, u32[]{:S(2)}, u32[]{:S(2)}) collective-permute-start(f32[320,256]{1,0:T(8,128)S(1)} %constant_dynamic-slice_fusion.37), channel_id=1, source_target_pairs={{0,1},{1,0},{2,3},{3,2},{4,5},{5,4},{6,7},{7,6},{8,9},{9,8},{10,11... | collective-permute-start | bytes 983048 | tf_op jit(solution)/shard_map/ppermute | solution.py:26
  609.2 3.2 collective-permute-start.108
  617.9 4.2 collective-permute-done.38
  622.1 3.1 collective-permute-start.39
  629.4 2.9 collective-permute-start.75
  635.8 11.7 %cholesky.164 = f32[128,128]{1,0:T(8,128)S(1)} custom-call(f32[128,128]{1,0:T(8,128)S(1)} %cholesky.197), custom_call_target="Cholesky" | custom-call | tf_op jit(solution)/shard_map/jit(cholesky)/cholesky | solution.py:107
  647.6 9.8 %custom-call.15 = f32[1,128,128]{1,2,0:T(8,128)S(1)} custom-call(f32[1,128,128]{2,1,0:T(8,128)S(1)} %get-tuple-element.121), custom_call_target="InvertDiagBlocksLowerTriangular" | custom-call | tf_op jit(solution)/shard_map/jit(cholesky)/cholesky | solution.py:107
  657.9 11.7 %cholesky.181 = f32[128,128]{1,0:T(8,128)S(1)} custom-call(f32[128,128]{1,0:T(8,128)S(1)} %convolution_subtract_fusion.3), custom_call_target="Cholesky" | custom-call | tf_op jit(solution)/shard_map/jit(cholesky)/cholesky | solution.py:107
  672.4 4.3 while.5
  676.7 19.7 %custom-call.16 = f32[2,128,128]{1,2,0:T(8,128)S(1)} custom-call(f32[2,128,128]{2,1,0:T(8,128)S(1)} %get-tuple-element.22), custom_call_target="InvertDiagBlocksLowerTriangular" | custom-call | tf_op jit(solution)/shard_map/triangular_solve/custom-call.0 | solution.py:108
  707.4 3.2 collective-permute-done.83
  710.7 4.2 collective-permute-start.84
  719.7 6.7 subtract_divide_fusion
  (465 shorter events, 243.4 us)
Async XLA Ops:
  15.3 15.4 %collective-permute-start.41 = (f32[192,256]{1,0:T(8,128)S(1)}, f32[192,256]{1,0:T(8,128)S(1)}, u32[]{:S(2)}, u32[]{:S(2)}) collective-permute-start(f32[192,256]{1,0:T(8,128)S(1)} %get-tuple-element.77), channel_id=1, source_target_pairs={{0,4},{1,5},{2,6},{3,7},{4,0},{5,1},{6,2},{7,3},{8,12},{9,13},{10,... | collective-permute-start | bytes 589832 | tf_op jit(solution)/shard_map/ppermute | solution.py:22
  18.2 14.7 %collective-permute-start.42 = (f32[192,256]{1,0:T(8,128)S(1)}, f32[192,256]{1,0:T(8,128)S(1)}, u32[]{:S(2)}, u32[]{:S(2)}) collective-permute-start(f32[192,256]{1,0:T(8,128)S(1)} %get-tuple-element.79), channel_id=1, source_target_pairs={{0,2},{1,3},{2,4},{3,5},{4,6},{5,7},{6,0},{7,1},{8,10},{9,11},{10,... | collective-permute-start | bytes 589832 | tf_op jit(solution)/shard_map/ppermute | solution.py:22
  18.5 14.4 %collective-permute-start.43 = (f32[192,256]{1,0:T(8,128)S(1)}, f32[192,256]{1,0:T(8,128)S(1)}, u32[]{:S(2)}, u32[]{:S(2)}) collective-permute-start(f32[192,256]{1,0:T(8,128)S(1)} %get-tuple-element.78), channel_id=1, source_target_pairs={{0,6},{1,7},{2,0},{3,1},{4,2},{5,3},{6,4},{7,5},{8,14},{9,15},{10,... | collective-permute-start | bytes 589832 | tf_op jit(solution)/shard_map/ppermute | solution.py:22
  30.2 12.1 %collective-permute-start.2 = (f32[192,256]{1,0:T(8,128)S(1)}, f32[192,256]{1,0:T(8,128)S(1)}, u32[]{:S(2)}, u32[]{:S(2)}) collective-permute-start(f32[192,256]{1,0:T(8,128)S(1)} %get-tuple-element.82), channel_id=1, source_target_pairs={{0,2},{1,3},{2,4},{3,5},{4,6},{5,7},{6,0},{7,1},{8,10},{9,11},{10,... | collective-permute-start | bytes 589832 | tf_op jit(solution)/shard_map/ppermute | solution.py:22
  30.8 11.5 %collective-permute-start.3 = (f32[192,256]{1,0:T(8,128)S(1)}, f32[192,256]{1,0:T(8,128)S(1)}, u32[]{:S(2)}, u32[]{:S(2)}) collective-permute-start(f32[192,256]{1,0:T(8,128)S(1)} %get-tuple-element.81), channel_id=1, source_target_pairs={{0,6},{1,7},{2,0},{3,1},{4,2},{5,3},{6,4},{7,5},{8,14},{9,15},{10,... | collective-permute-start | bytes 589832 | tf_op jit(solution)/shard_map/ppermute | solution.py:22
  33.1 14.5 %collective-permute-start.44 = (f32[192,256]{1,0:T(8,128)S(1)}, f32[192,256]{1,0:T(8,128)S(1)}, u32[]{:S(2)}, u32[]{:S(2)}) collective-permute-start(f32[192,256]{1,0:T(8,128)S(1)} %get-tuple-element.46), channel_id=1, source_target_pairs={{0,2},{1,3},{2,4},{3,5},{4,6},{5,7},{6,0},{7,1},{8,10},{9,11},{10,... | collective-permute-start | bytes 589832 | tf_op jit(solution)/shard_map/ppermute | solution.py:22
  33.2 14.5 %collective-permute-start.45 = (f32[192,256]{1,0:T(8,128)S(1)}, f32[192,256]{1,0:T(8,128)S(1)}, u32[]{:S(2)}, u32[]{:S(2)}) collective-permute-start(f32[192,256]{1,0:T(8,128)S(1)} %get-tuple-element.46), channel_id=1, source_target_pairs={{0,6},{1,7},{2,0},{3,1},{4,2},{5,3},{6,4},{7,5},{8,14},{9,15},{10,... | collective-permute-start | bytes 589832 | tf_op jit(solution)/shard_map/ppermute | solution.py:22
  37.0 12.6 %collective-permute-start.46 = (f32[192,256]{1,0:T(8,128)S(1)}, f32[192,256]{1,0:T(8,128)S(1)}, u32[]{:S(2)}, u32[]{:S(2)}) collective-permute-start(f32[192,256]{1,0:T(8,128)S(1)} %get-tuple-element.46), channel_id=1, source_target_pairs={{0,4},{1,5},{2,6},{3,7},{4,0},{5,1},{6,2},{7,3},{8,12},{9,13},{10,... | collective-permute-start | bytes 589832 | tf_op jit(solution)/shard_map/ppermute | solution.py:22
  43.1 14.4 %collective-permute-start.4 = (f32[192,256]{1,0:T(8,128)}, f32[192,256]{1,0:T(8,128)}, u32[]{:S(2)}, u32[]{:S(2)}) collective-permute-start(f32[192,256]{1,0:T(8,128)} %get-tuple-element.48), channel_id=1, source_target_pairs={{0,2},{1,3},{2,4},{3,5},{4,6},{5,7},{6,0},{7,1},{8,10},{9,11},{10,... | collective-permute-start | bytes 589832 | tf_op jit(solution)/shard_map/ppermute | solution.py:22
  49.6 17.1 %collective-permute-start.47 = (f32[768,256]{1,0:T(8,128)S(1)}, f32[768,256]{1,0:T(8,128)S(1)}, u32[]{:S(2)}, u32[]{:S(2)}) collective-permute-start(f32[768,256]{1,0:T(8,128)S(1)} %constant_dynamic-update-slice_fusion.30), channel_id=1, source_target_pairs={{0,1},{1,0},{2,3},{3,2},{4,5},{5,4},{6,7},{7,6},{8,9},{9,8},{10,11... | collective-permute-start | bytes 2359304 | tf_op jit(solution)/shard_map/ppermute | solution.py:26
  57.5 8.2 %collective-permute-start.6 = (f32[192,256]{1,0:T(8,128)}, f32[192,256]{1,0:T(8,128)S(1)}, u32[]{:S(2)}, u32[]{:S(2)}) collective-permute-start(f32[192,256]{1,0:T(8,128)} %get-tuple-element.48), channel_id=1, source_target_pairs={{0,4},{1,5},{2,6},{3,7},{4,0},{5,1},{6,2},{7,3},{8,12},{9,13},{10,... | collective-permute-start | bytes 589832 | tf_op jit(solution)/shard_map/ppermute | solution.py:22
  77.8 18.5 %collective-permute-start.48 = (f32[96,256]{1,0:T(8,128)S(1)}, f32[96,256]{1,0:T(8,128)S(1)}, u32[]{:S(2)}, u32[]{:S(2)}) collective-permute-start(f32[96,256]{1,0:T(8,128)S(1)} %get-tuple-element.99), channel_id=1, source_target_pairs={{0,16},{8,24},{16,0},{24,8},{32,48},{40,56},{48,32},{56,40},{64,80... | collective-permute-start | bytes 294920 | tf_op jit(solution)/shard_map/ppermute | solution.py:22
  80.8 17.5 %collective-permute-start.49 = (f32[96,256]{1,0:T(8,128)S(1)}, f32[96,256]{1,0:T(8,128)S(1)}, u32[]{:S(2)}, u32[]{:S(2)}) collective-permute-start(f32[96,256]{1,0:T(8,128)S(1)} %get-tuple-element.101), channel_id=1, source_target_pairs={{0,8},{8,16},{16,24},{24,0},{32,40},{40,48},{48,56},{56,32},{64,72... | collective-permute-start | bytes 294920 | tf_op jit(solution)/shard_map/ppermute | solution.py:22
  81.2 17.1 %collective-permute-start.50 = (f32[96,256]{1,0:T(8,128)S(1)}, f32[96,256]{1,0:T(8,128)S(1)}, u32[]{:S(2)}, u32[]{:S(2)}) collective-permute-start(f32[96,256]{1,0:T(8,128)S(1)} %get-tuple-element.100), channel_id=1, source_target_pairs={{0,24},{8,0},{16,8},{24,16},{32,56},{40,32},{48,40},{56,48},{64,88... | collective-permute-start | bytes 294920 | tf_op jit(solution)/shard_map/ppermute | solution.py:22
  83.5 15.9 %collective-permute-start.54 = (f32[96,256]{1,0:T(8,128)S(1)}, f32[96,256]{1,0:T(8,128)S(1)}, u32[]{:S(2)}, u32[]{:S(2)}) collective-permute-start(f32[96,256]{1,0:T(8,128)S(1)} %get-tuple-element.102), channel_id=1, source_target_pairs={{0,64},{8,72},{16,80},{24,88},{32,96},{40,104},{48,112},{56,120},{... | collective-permute-start | bytes 294920 | tf_op jit(solution)/shard_map/ppermute | solution.py:22
  87.1 12.3 %collective-permute-start.55 = (f32[96,256]{1,0:T(8,128)S(1)}, f32[96,256]{1,0:T(8,128)S(1)}, u32[]{:S(2)}, u32[]{:S(2)}) collective-permute-start(f32[96,256]{1,0:T(8,128)S(1)} %get-tuple-element.104), channel_id=1, source_target_pairs={{0,32},{8,40},{16,48},{24,56},{32,64},{40,72},{48,80},{56,88},{64,... | collective-permute-start | bytes 294920 | tf_op jit(solution)/shard_map/ppermute | solution.py:22
  98.3 41.9 %collective-permute-start.10 = (f32[32,3200]{1,0:T(8,128)S(1)}, f32[32,3200]{1,0:T(8,128)S(1)}, u32[]{:S(2)}, u32[]{:S(2)}) collective-permute-start(f32[32,3200]{1,0:T(8,128)S(1)} %get-tuple-element.61), channel_id=1, source_target_pairs={{0,24},{8,0},{16,8},{24,16},{32,56},{40,32},{48,40},{56,48},{64,88... | collective-permute-start | bytes 1228808 | tf_op jit(solution)/shard_map/ppermute | solution.py:22
  98.3 47.9 %collective-permute-start.8 = (f32[32,3200]{1,0:T(8,128)S(1)}, f32[32,3200]{1,0:T(8,128)S(1)}, u32[]{:S(2)}, u32[]{:S(2)}) collective-permute-start(f32[32,3200]{1,0:T(8,128)S(1)} %get-tuple-element.60), channel_id=1, source_target_pairs={{0,16},{8,24},{16,0},{24,8},{32,48},{40,56},{48,32},{56,40},{64,80... | collective-permute-start | bytes 1228808 | tf_op jit(solution)/shard_map/ppermute | solution.py:22
  105.7 10.8 %collective-permute-start.58 = (f32[24,256]{1,0:T(8,128)S(1)}, f32[24,256]{1,0:T(8,128)S(1)}, u32[]{:S(2)}, u32[]{:S(2)}) collective-permute-start(f32[24,256]{1,0:T(8,128)S(1)} %get-tuple-element.116), channel_id=1, source_target_pairs={{0,8},{8,16},{16,24},{24,0},{32,40},{40,48},{48,56},{56,32},{64,72... | collective-permute-start | bytes 73736 | tf_op jit(solution)/shard_map/ppermute | solution.py:22
  107.3 9.8 %collective-permute-start.59 = (f32[24,256]{1,0:T(8,128)S(1)}, f32[24,256]{1,0:T(8,128)S(1)}, u32[]{:S(2)}, u32[]{:S(2)}) collective-permute-start(f32[24,256]{1,0:T(8,128)S(1)} %get-tuple-element.115), channel_id=1, source_target_pairs={{0,24},{8,0},{16,8},{24,16},{32,56},{40,32},{48,40},{56,48},{64,88... | collective-permute-start | bytes 73736 | tf_op jit(solution)/shard_map/ppermute | solution.py:22
  109.7 41.8 %collective-permute-start.9 = (f32[32,3200]{1,0:T(8,128)S(1)}, f32[32,3200]{1,0:T(8,128)S(1)}, u32[]{:S(2)}, u32[]{:S(2)}) collective-permute-start(f32[32,3200]{1,0:T(8,128)S(1)} %get-tuple-element.62), channel_id=1, source_target_pairs={{0,8},{8,16},{16,24},{24,0},{32,40},{40,48},{48,56},{56,32},{64,72... | collective-permute-start | bytes 1228808 | tf_op jit(solution)/shard_map/ppermute | solution.py:22
  117.1 9.9 %collective-permute-start.60 = (f32[48,256]{1,0:T(8,128)S(1)}, f32[48,256]{1,0:T(8,128)S(1)}, u32[]{:S(2)}, u32[]{:S(2)}) collective-permute-start(f32[48,256]{1,0:T(8,128)S(1)} %pad_maximum_fusion.18), channel_id=1, source_target_pairs={{0,0},{1,16},{2,32},{3,48},{4,64},{5,80},{6,96},{7,112},{8,2},{9,1... | collective-permute-start | bytes 147464 | tf_op jit(solution)/shard_map/ppermute | solution.py:154
  125.6 27.4 %collective-permute-start.20 = (f32[32,3200]{1,0:T(8,128)S(1)}, f32[32,3200]{1,0:T(8,128)S(1)}, u32[]{:S(2)}, u32[]{:S(2)}) collective-permute-start(f32[32,3200]{1,0:T(8,128)S(1)} %get-tuple-element.57), channel_id=1, source_target_pairs={{0,64},{8,72},{16,80},{24,88},{32,96},{40,104},{48,112},{56,120},{... | collective-permute-start | bytes 1228808 | tf_op jit(solution)/shard_map/ppermute | solution.py:22
  140.2 13.8 %collective-permute-start.21 = (f32[32,3200]{1,0:T(8,128)S(1)}, f32[32,3200]{1,0:T(8,128)S(1)}, u32[]{:S(2)}, u32[]{:S(2)}) collective-permute-start(f32[32,3200]{1,0:T(8,128)S(1)} %get-tuple-element.59), channel_id=1, source_target_pairs={{0,32},{8,40},{16,48},{24,56},{32,64},{40,72},{48,80},{56,88},{64,... | collective-permute-start | bytes 1228808 | tf_op jit(solution)/shard_map/ppermute | solution.py:22
  140.2 13.8 %collective-permute-start.22 = (f32[32,3200]{1,0:T(8,128)S(1)}, f32[32,3200]{1,0:T(8,128)S(1)}, u32[]{:S(2)}, u32[]{:S(2)}) collective-permute-start(f32[32,3200]{1,0:T(8,128)S(1)} %get-tuple-element.58), channel_id=1, source_target_pairs={{0,96},{8,104},{16,112},{24,120},{32,0},{40,8},{48,16},{56,24},{64... | collective-permute-start | bytes 1228808 | tf_op jit(solution)/shard_map/ppermute | solution.py:22
  151.6 14.1 %collective-permute-start.11 = (f32[8,3200]{1,0:T(8,128)S(1)}, f32[8,3200]{1,0:T(8,128)S(1)}, u32[]{:S(2)}, u32[]{:S(2)}) collective-permute-start(f32[8,3200]{1,0:T(8,128)S(1)} %get-tuple-element.88), channel_id=1, source_target_pairs={{0,64},{8,72},{16,80},{24,88},{32,96},{40,104},{48,112},{56,120},{... | collective-permute-start | bytes 307208 | tf_op jit(solution)/shard_map/ppermute | solution.py:22
  153.0 15.5 %collective-permute-start.12 = (f32[8,3200]{1,0:T(8,128)S(1)}, f32[8,3200]{1,0:T(8,128)S(1)}, u32[]{:S(2)}, u32[]{:S(2)}) collective-permute-start(f32[8,3200]{1,0:T(8,128)S(1)} %get-tuple-element.90), channel_id=1, source_target_pairs={{0,32},{8,40},{16,48},{24,56},{32,64},{40,72},{48,80},{56,88},{64,... | collective-permute-start | bytes 307208 | tf_op jit(solution)/shard_map/ppermute | solution.py:22
  155.0 8.9 %collective-permute-start.66 = (f32[72,256]{0,1:T(8,128)S(1)}, f32[72,256]{0,1:T(8,128)S(1)}, u32[]{:S(2)}, u32[]{:S(2)}) collective-permute-start(f32[72,256]{0,1:T(8,128)S(1)} %maximum_maximum_fusion), channel_id=1, source_target_pairs={{0,8},{8,16},{16,24},{24,0},{32,40},{40,48},{48,56},{56,32},{64,72... | collective-permute-start | bytes 221192 | tf_op jit(solution)/shard_map/ppermute | solution.py:22
  155.1 10.5 %collective-permute-start.67 = (f32[72,256]{0,1:T(8,128)S(1)}, f32[72,256]{0,1:T(8,128)S(1)}, u32[]{:S(2)}, u32[]{:S(2)}) collective-permute-start(f32[72,256]{0,1:T(8,128)S(1)} %maximum_maximum_fusion), channel_id=1, source_target_pairs={{0,24},{8,0},{16,8},{24,16},{32,56},{40,32},{48,40},{56,48},{64,88... | collective-permute-start | bytes 221192 | tf_op jit(solution)/shard_map/ppermute | solution.py:22
  175.8 34.3 %collective-permute-start.16 = (f32[8,3200]{1,0:T(8,128)}, f32[8,3200]{1,0:T(8,128)}, u32[]{:S(2)}, u32[]{:S(2)}) collective-permute-start(f32[8,3200]{1,0:T(8,128)} %add_add_fusion.9), channel_id=1, source_target_pairs={{0,64},{8,72},{16,80},{24,88},{32,96},{40,104},{48,112},{56,120},{... | collective-permute-start | bytes 307208 | tf_op jit(solution)/shard_map/ppermute | solution.py:22
  175.9 38.1 %collective-permute-start.26 = (f32[8,3200]{1,0:T(8,128)}, f32[8,3200]{1,0:T(8,128)}, u32[]{:S(2)}, u32[]{:S(2)}) collective-permute-start(f32[8,3200]{1,0:T(8,128)} %add_add_fusion.8), channel_id=1, source_target_pairs={{0,8},{8,16},{16,24},{24,0},{32,40},{40,48},{48,56},{56,32},{64,72... | collective-permute-start | bytes 307208 | tf_op jit(solution)/shard_map/ppermute | solution.py:22
  175.9 38.1 %collective-permute-start.27 = (f32[8,3200]{1,0:T(8,128)}, f32[8,3200]{1,0:T(8,128)}, u32[]{:S(2)}, u32[]{:S(2)}) collective-permute-start(f32[8,3200]{1,0:T(8,128)} %add_add_fusion.8), channel_id=1, source_target_pairs={{0,24},{8,0},{16,8},{24,16},{32,56},{40,32},{48,40},{56,48},{64,88... | collective-permute-start | bytes 307208 | tf_op jit(solution)/shard_map/ppermute | solution.py:22
  178.6 38.1 %collective-permute-start.28 = (f32[8,3200]{1,0:T(8,128)}, f32[8,3200]{1,0:T(8,128)}, u32[]{:S(2)}, u32[]{:S(2)}) collective-permute-start(f32[8,3200]{1,0:T(8,128)} %add_add_fusion.8), channel_id=1, source_target_pairs={{0,16},{8,24},{16,0},{24,8},{32,48},{40,56},{48,32},{56,40},{64,80... | collective-permute-start | bytes 307208 | tf_op jit(solution)/shard_map/ppermute | solution.py:22
  179.9 39.5 %collective-permute-start.71 = (f32[72,256]{0,1:T(8,128)S(1)}, f32[72,256]{0,1:T(8,128)}, u32[]{:S(2)}, u32[]{:S(2)}) collective-permute-start(f32[72,256]{0,1:T(8,128)S(1)} %add_add_fusion.6), channel_id=1, source_target_pairs={{0,2},{1,3},{2,4},{3,5},{4,6},{5,7},{6,0},{7,1},{8,10},{9,11},{10,... | collective-permute-start | bytes 221192 | tf_op jit(solution)/shard_map/ppermute | solution.py:22
  210.2 141.9 %collective-permute-start.85 = (f32[32,3072]{1,0:T(8,128)}, f32[32,3072]{1,0:T(8,128)}, u32[]{:S(2)}, u32[]{:S(2)}) collective-permute-start(f32[32,3072]{1,0:T(8,128)} %get-tuple-element.63), channel_id=1, source_target_pairs={{0,16},{8,24},{16,0},{24,8},{32,48},{40,56},{48,32},{56,40},{64,80... | collective-permute-start | bytes 1179656 | tf_op jit(solution)/shard_map/ppermute | solution.py:22
  214.0 141.2 %collective-permute-start.86 = (f32[32,3072]{1,0:T(8,128)}, f32[32,3072]{1,0:T(8,128)}, u32[]{:S(2)}, u32[]{:S(2)}) collective-permute-start(f32[32,3072]{1,0:T(8,128)} %get-tuple-element.65), channel_id=1, source_target_pairs={{0,8},{8,16},{16,24},{24,0},{32,40},{40,48},{48,56},{56,32},{64,72... | collective-permute-start | bytes 1179656 | tf_op jit(solution)/shard_map/ppermute | solution.py:22
  214.0 141.2 %collective-permute-start.87 = (f32[32,3072]{1,0:T(8,128)}, f32[32,3072]{1,0:T(8,128)}, u32[]{:S(2)}, u32[]{:S(2)}) collective-permute-start(f32[32,3072]{1,0:T(8,128)} %get-tuple-element.64), channel_id=1, source_target_pairs={{0,24},{8,0},{16,8},{24,16},{32,56},{40,32},{48,40},{56,48},{64,88... | collective-permute-start | bytes 1179656 | tf_op jit(solution)/shard_map/ppermute | solution.py:22
  216.7 124.8 %collective-permute-start.72 = (f32[72,256]{0,1:T(8,128)S(1)}, f32[72,256]{0,1:T(8,128)}, u32[]{:S(2)}, u32[]{:S(2)}) collective-permute-start(f32[72,256]{0,1:T(8,128)S(1)} %add_add_fusion.6), channel_id=1, source_target_pairs={{0,6},{1,7},{2,0},{3,1},{4,2},{5,3},{6,4},{7,5},{8,14},{9,15},{10,... | collective-permute-start | bytes 221192 | tf_op jit(solution)/shard_map/ppermute | solution.py:22
  219.4 128.1 %collective-permute-start.73 = (f32[72,256]{0,1:T(8,128)S(1)}, f32[72,256]{0,1:T(8,128)}, u32[]{:S(2)}, u32[]{:S(2)}) collective-permute-start(f32[72,256]{0,1:T(8,128)S(1)} %add_add_fusion.6), channel_id=1, source_target_pairs={{0,4},{1,5},{2,6},{3,7},{4,0},{5,1},{6,2},{7,3},{8,12},{9,13},{10,... | collective-permute-start | bytes 221192 | tf_op jit(solution)/shard_map/ppermute | solution.py:22
  341.5 17.9 %collective-permute-start.97 = (f32[32,3072]{1,0:T(8,128)}, f32[32,3072]{1,0:T(8,128)}, u32[]{:S(2)}, u32[]{:S(2)}) collective-permute-start(f32[32,3072]{1,0:T(8,128)} %get-tuple-element.66), channel_id=1, source_target_pairs={{0,64},{8,72},{16,80},{24,88},{32,96},{40,104},{48,112},{56,120},{... | collective-permute-start | bytes 1179656 | tf_op jit(solution)/shard_map/ppermute | solution.py:22
  347.4 12.1 %collective-permute-start.98 = (f32[32,3072]{1,0:T(8,128)}, f32[32,3072]{1,0:T(8,128)}, u32[]{:S(2)}, u32[]{:S(2)}) collective-permute-start(f32[32,3072]{1,0:T(8,128)} %get-tuple-element.68), channel_id=1, source_target_pairs={{0,32},{8,40},{16,48},{24,56},{32,64},{40,72},{48,80},{56,88},{64,... | collective-permute-start | bytes 1179656 | tf_op jit(solution)/shard_map/ppermute | solution.py:22
  352.1 13.4 %collective-permute-start.99 = (f32[32,3072]{1,0:T(8,128)}, f32[32,3072]{1,0:T(8,128)S(1)}, u32[]{:S(2)}, u32[]{:S(2)}) collective-permute-start(f32[32,3072]{1,0:T(8,128)} %get-tuple-element.67), channel_id=1, source_target_pairs={{0,96},{8,104},{16,112},{24,120},{32,0},{40,8},{48,16},{56,24},{64... | collective-permute-start | bytes 1179656 | tf_op jit(solution)/shard_map/ppermute | solution.py:22
  355.2 126.1 %collective-permute-start.17 = (f32[32,3200]{1,0:T(8,128)}, f32[32,3200]{1,0:T(8,128)}, u32[]{:S(2)}, u32[]{:S(2)}) collective-permute-start(f32[32,3200]{1,0:T(8,128)} %copy.37), channel_id=1, source_target_pairs={{0,8},{8,16},{16,24},{24,0},{32,40},{40,48},{48,56},{56,32},{64,72... | collective-permute-start | bytes 1228808 | tf_op jit(solution)/shard_map/ppermute | solution.py:22
  355.2 145.8 %collective-permute-start.18 = (f32[32,3200]{1,0:T(8,128)}, f32[32,3200]{1,0:T(8,128)}, u32[]{:S(2)}, u32[]{:S(2)}) collective-permute-start(f32[32,3200]{1,0:T(8,128)} %copy.37), channel_id=1, source_target_pairs={{0,24},{8,0},{16,8},{24,16},{32,56},{40,32},{48,40},{56,48},{64,88... | collective-permute-start | bytes 1228808 | tf_op jit(solution)/shard_map/ppermute | solution.py:22
  359.4 10.4 %collective-permute-start.88 = (f32[8,3072]{1,0:T(8,128)S(1)}, f32[8,3072]{1,0:T(8,128)S(1)}, u32[]{:S(2)}, u32[]{:S(2)}) collective-permute-start(f32[8,3072]{1,0:T(8,128)S(1)} %get-tuple-element.91), channel_id=1, source_target_pairs={{0,64},{8,72},{16,80},{24,88},{32,96},{40,104},{48,112},{56,120},{... | collective-permute-start | bytes 294920 | tf_op jit(solution)/shard_map/ppermute | solution.py:22
  359.5 10.4 %collective-permute-start.89 = (f32[8,3072]{1,0:T(8,128)S(1)}, f32[8,3072]{1,0:T(8,128)S(1)}, u32[]{:S(2)}, u32[]{:S(2)}) collective-permute-start(f32[8,3072]{1,0:T(8,128)S(1)} %get-tuple-element.93), channel_id=1, source_target_pairs={{0,32},{8,40},{16,48},{24,56},{32,64},{40,72},{48,80},{56,88},{64,... | collective-permute-start | bytes 294920 | tf_op jit(solution)/shard_map/ppermute | solution.py:22
  375.9 142.1 %collective-permute-start.19 = (f32[32,3200]{1,0:T(8,128)}, f32[32,3200]{1,0:T(8,128)}, u32[]{:S(2)}, u32[]{:S(2)}) collective-permute-start(f32[32,3200]{1,0:T(8,128)} %copy.37), channel_id=1, source_target_pairs={{0,16},{8,24},{16,0},{24,8},{32,48},{40,56},{48,32},{56,40},{64,80... | collective-permute-start | bytes 1228808 | tf_op jit(solution)/shard_map/ppermute | solution.py:22
  377.1 158.9 %collective-permute-start.29 = (f32[32,3200]{1,0:T(8,128)}, f32[32,3200]{1,0:T(8,128)}, u32[]{:S(2)}, u32[]{:S(2)}) collective-permute-start(f32[32,3200]{1,0:T(8,128)} %copy.47), channel_id=1, source_target_pairs={{0,32},{8,40},{16,48},{24,56},{32,64},{40,72},{48,80},{56,88},{64,... | collective-permute-start | bytes 1228808 | tf_op jit(solution)/shard_map/ppermute | solution.py:22
  377.1 12.1 %collective-permute-start.74 = (f32[288,256]{1,0:T(8,128)}, f32[288,256]{1,0:T(8,128)S(1)}, u32[]{:S(2)}, u32[]{:S(2)}) collective-permute-start(f32[288,256]{1,0:T(8,128)} %constant_dynamic-update-slice_fusion.22), channel_id=1, source_target_pairs={{0,1},{1,0},{2,3},{3,2},{4,5},{5,4},{6,7},{7,6},{8,9},{9,8},{10,11... | collective-permute-start | bytes 884744 | tf_op jit(solution)/shard_map/ppermute | solution.py:26
  389.3 65.3 %collective-permute-start.91 = (f32[8,3072]{1,0:T(8,128)}, f32[8,3072]{1,0:T(8,128)S(1)}, u32[]{:S(2)}, u32[]{:S(2)}) collective-permute-start(f32[8,3072]{1,0:T(8,128)} %get-tuple-element.40), channel_id=1, source_target_pairs={{0,32},{8,40},{16,48},{24,56},{32,64},{40,72},{48,80},{56,88},{64,... | collective-permute-start | bytes 294920 | tf_op jit(solution)/shard_map/ppermute | solution.py:22
  478.0 72.0 %collective-permute-start.30 = (f32[32,3200]{1,0:T(8,128)}, f32[32,3200]{1,0:T(8,128)}, u32[]{:S(2)}, u32[]{:S(2)}) collective-permute-start(f32[32,3200]{1,0:T(8,128)} %copy.47), channel_id=1, source_target_pairs={{0,96},{8,104},{16,112},{24,120},{32,0},{40,8},{48,16},{56,24},{64... | collective-permute-start | bytes 1228808 | tf_op jit(solution)/shard_map/ppermute | solution.py:22
  481.3 82.1 %collective-permute-start.31 = (f32[32,3200]{1,0:T(8,128)}, f32[32,3200]{1,0:T(8,128)S(1)}, u32[]{:S(2)}, u32[]{:S(2)}) collective-permute-start(f32[32,3200]{1,0:T(8,128)} %copy.47), channel_id=1, source_target_pairs={{0,64},{8,72},{16,80},{24,88},{32,96},{40,104},{48,112},{56,120},{... | collective-permute-start | bytes 1228808 | tf_op jit(solution)/shard_map/ppermute | solution.py:22
  501.0 98.3 %collective-permute-start.94 = (f32[32,3072]{1,0:T(8,128)S(1)}, f32[32,3072]{1,0:T(8,128)}, u32[]{:S(2)}, u32[]{:S(2)}) collective-permute-start(f32[32,3072]{1,0:T(8,128)S(1)} %constant_dynamic-update-slice_fusion.14), channel_id=1, source_target_pairs={{0,8},{8,16},{16,24},{24,0},{32,40},{40,48},{48,56},{56,32},{64,72... | collective-permute-start | bytes 1179656 | tf_op jit(solution)/shard_map/ppermute | solution.py:22
  518.0 84.9 %collective-permute-start.95 = (f32[32,3072]{1,0:T(8,128)S(1)}, f32[32,3072]{1,0:T(8,128)}, u32[]{:S(2)}, u32[]{:S(2)}) collective-permute-start(f32[32,3072]{1,0:T(8,128)S(1)} %constant_dynamic-update-slice_fusion.14), channel_id=1, source_target_pairs={{0,24},{8,0},{16,8},{24,16},{32,56},{40,32},{48,40},{56,48},{64,88... | collective-permute-start | bytes 1179656 | tf_op jit(solution)/shard_map/ppermute | solution.py:22
  536.1 68.7 %collective-permute-start.96 = (f32[32,3072]{1,0:T(8,128)S(1)}, f32[32,3072]{1,0:T(8,128)}, u32[]{:S(2)}, u32[]{:S(2)}) collective-permute-start(f32[32,3072]{1,0:T(8,128)S(1)} %constant_dynamic-update-slice_fusion.14), channel_id=1, source_target_pairs={{0,16},{8,24},{16,0},{24,8},{32,48},{40,56},{48,32},{56,40},{64,80... | collective-permute-start | bytes 1179656 | tf_op jit(solution)/shard_map/ppermute | solution.py:22
  550.0 65.3 %collective-permute-start.106 = (f32[32,3072]{1,0:T(8,128)}, f32[32,3072]{1,0:T(8,128)}, u32[]{:S(2)}, u32[]{:S(2)}) collective-permute-start(f32[32,3072]{1,0:T(8,128)} %constant_dynamic-update-slice_fusion.6), channel_id=1, source_target_pairs={{0,32},{8,40},{16,48},{24,56},{32,64},{40,72},{48,80},{56,88},{64,... | collective-permute-start | bytes 1179656 | tf_op jit(solution)/shard_map/ppermute | solution.py:22
  588.0 9.6 %collective-permute-start.32 = (f32[320,256]{1,0:T(8,128)S(1)}, f32[320,256]{1,0:T(8,128)S(1)}, u32[]{:S(2)}, u32[]{:S(2)}) collective-permute-start(f32[320,256]{1,0:T(8,128)S(1)} %constant_dynamic-slice_fusion.37), channel_id=1, source_target_pairs={{0,1},{1,0},{2,3},{3,2},{4,5},{5,4},{6,7},{7,6},{8,9},{9,8},{10,11... | collective-permute-start | bytes 983048 | tf_op jit(solution)/shard_map/ppermute | solution.py:26
  597.7 27.6 %collective-permute-start.107 = (f32[32,3072]{1,0:T(8,128)}, f32[32,3072]{1,0:T(8,128)S(1)}, u32[]{:S(2)}, u32[]{:S(2)}) collective-permute-start(f32[32,3072]{1,0:T(8,128)} %constant_dynamic-update-slice_fusion.6), channel_id=1, source_target_pairs={{0,96},{8,104},{16,112},{24,120},{32,0},{40,8},{48,16},{56,24},{64... | collective-permute-start | bytes 1179656 | tf_op jit(solution)/shard_map/ppermute | solution.py:22
  599.3 9.9 %collective-permute-start.33 = (f32[80,256]{1,0:T(8,128)S(1)}, f32[80,256]{1,0:T(8,128)S(1)}, u32[]{:S(2)}, u32[]{:S(2)}) collective-permute-start(f32[80,256]{1,0:T(8,128)S(1)} %get-tuple-element.105), channel_id=1, source_target_pairs={{0,4},{1,5},{2,6},{3,7},{4,0},{5,1},{6,2},{7,3},{8,12},{9,13},{10,... | collective-permute-start | bytes 245768 | tf_op jit(solution)/shard_map/ppermute | solution.py:22
  602.9 9.4 %collective-permute-start.34 = (f32[80,256]{1,0:T(8,128)S(1)}, f32[80,256]{1,0:T(8,128)S(1)}, u32[]{:S(2)}, u32[]{:S(2)}) collective-permute-start(f32[80,256]{1,0:T(8,128)S(1)} %get-tuple-element.107), channel_id=1, source_target_pairs={{0,2},{1,3},{2,4},{3,5},{4,6},{5,7},{6,0},{7,1},{8,10},{9,11},{10,... | collective-permute-start | bytes 245768 | tf_op jit(solution)/shard_map/ppermute | solution.py:22
  609.2 16.1 %collective-permute-start.108 = (f32[32,3072]{1,0:T(8,128)}, f32[32,3072]{1,0:T(8,128)S(1)}, u32[]{:S(2)}, u32[]{:S(2)}) collective-permute-start(f32[32,3072]{1,0:T(8,128)} %constant_dynamic-update-slice_fusion.6), channel_id=1, source_target_pairs={{0,64},{8,72},{16,80},{24,88},{32,96},{40,104},{48,112},{56,120},{... | collective-permute-start | bytes 1179656 | tf_op jit(solution)/shard_map/ppermute | solution.py:22
  629.4 67.0 %collective-permute-start.75 = (f32[32,256]{1,0:T(8,128)}, f32[32,256]{1,0:T(8,128)S(1)}, u32[]{:S(2)}, u32[]{:S(2)}) collective-permute-start(f32[32,256]{1,0:T(8,128)} %constant_dynamic-slice_fusion.14), channel_id=1, source_target_pairs={{0,16},{8,24},{16,0},{24,8},{32,48},{40,56},{48,32},{56,40},{64,80... | collective-permute-start | bytes 98312 | tf_op jit(solution)/shard_map/ppermute | solution.py:22
  632.3 64.2 %collective-permute-start.76 = (f32[32,256]{1,0:T(8,128)}, f32[32,256]{1,0:T(8,128)S(1)}, u32[]{:S(2)}, u32[]{:S(2)}) collective-permute-start(f32[32,256]{1,0:T(8,128)} %constant_dynamic-slice_fusion.14), channel_id=1, source_target_pairs={{0,8},{8,16},{16,24},{24,0},{32,40},{40,48},{48,56},{56,32},{64,72... | collective-permute-start | bytes 98312 | tf_op jit(solution)/shard_map/ppermute | solution.py:22
  632.4 64.1 %collective-permute-start.77 = (f32[32,256]{1,0:T(8,128)}, f32[32,256]{1,0:T(8,128)}, u32[]{:S(2)}, u32[]{:S(2)}) collective-permute-start(f32[32,256]{1,0:T(8,128)} %constant_dynamic-slice_fusion.14), channel_id=1, source_target_pairs={{0,24},{8,0},{16,8},{24,16},{32,56},{40,32},{48,40},{56,48},{64,88... | collective-permute-start | bytes 98312 | tf_op jit(solution)/shard_map/ppermute | solution.py:22
  (82 other events, 761.2 us)
